TPU v7x, 32 devices: a whole 2x2x4 slice. The times are simulated.
32 devices in a mesh: groups: 2 (over y), lat: 4 (over z), lon: 2 (over x), feat: 2 (over core).
Axes of the slice: x: 2, y: 2, z: 4, core: 2. Of those that a mesh axis runs over, the one named last changes fastest.
Arguments:
- grid_latent: bfloat16 [32768, 512], P(('groups', 'lat', 'lon'), 'feat'), parts along dimension 0, may hold values from -6 to 6
- teacher: bfloat16 [32768, 512], P(('groups', 'lat', 'lon'), 'feat'), parts along dimension 0, may hold values from -6 to 6
- mesh_init: bfloat16 [5120, 512], P(('groups', 'lat', 'lon'), 'feat'), parts along dimension 0, may hold values from -6 to 6
- enc_weight: bfloat16 [512, 512], P(None, 'feat'), may hold values from -0.25 to 0.25
- proc_weight: bfloat16 [512, 512], P(None, 'feat'), may hold values from -0.25 to 0.25
- dec_weight: bfloat16 [512, 512], P(None, 'feat'), may hold values from -0.25 to 0.25
- local_grid: int32 [16384], P(('lat', 'lon')), may hold values from 0 to 2047
- local_mesh: int32 [16384], P(('lat', 'lon')), may hold values from 0 to 319
- local_weight: float32 [16384], P(('lat', 'lon')), may hold values from 0.2 to 1
- send_row: int32 [40, 256], P(('lat', 'lon')), may hold values from 0 to 2047
- send_count: int32 [40], P(('lat', 'lon')), may hold values from 0 to 256, as said below
- recv_row: int32 [40, 256], P(('lat', 'lon')), may hold values from 0 to 319
- recv_weight: float32 [40, 256], P(('lat', 'lon')), may hold values from 0.2 to 1
- coarse_index: int32 [2560, 2], P(('lat', 'lon')), may hold values from 0 to 31
- coarse_weight: float32 [2560, 2], P(('lat', 'lon')), may hold values from -3 to 3
Outputs:
- loss_value: float32 [2], P('groups'), parts along dimension 0
- grad_x: bfloat16 [32768, 512], P(('groups', 'lat', 'lon'), 'feat'), parts along dimension 0
- grad_dec: float32 [1024, 512], P(('groups', 'lat', 'lon'), 'feat'), parts along dimension 0
There are 2 independent parts, one for each index of `groups`. A program takes and returns all parts, laid end to end along the dimension named above; an argument that names none is the same for every part. Nothing has to cross between parts.
Inputs may be any that keep to these rules, and one draw needn't show every extreme that they name: send_count[s * 5 + k] is 0 exactly where the target band of neighbour k does not exist; otherwise at least 1. The bucket to neighbour (0,1) and every bucket of the first and last bands are full wherever the target exists.
All inputs are finite; a program needn't handle non-finite values.
Results may differ from a plain program's by a relative error of at most 0.0067.
Values may be sent and summed in bfloat16 or wider, within the bound.
A program may use at most 64 MiB of HBM per device.

v0:
```python
import jax
import jax.numpy as jnp
from jax import lax
from jax.sharding import PartitionSpec as P

CDEV = 4


OFFSETS = ((-1, 0), (1, 0), (-1, 1), (0, 1), (1, 1))


def passed_along(x, axis, by):
    length = lax.axis_size(axis)
    pairs = [(i, i + by) for i in range(length) if 0 <= i + by < length]
    return lax.ppermute(x, axis, pairs)


def shifted(x, axis, by):
    length = lax.axis_size(axis)
    return lax.ppermute(x, axis, [(i, (i + by) % length) for i in range(length)])


def silu_slope(pre_value):
    sigma = jax.nn.sigmoid(pre_value)
    return sigma * (1.0 + pre_value * (1.0 - sigma))


def project(values, local_cols):
    widened = lax.all_gather(values, "feat", axis=1, tiled=True)
    return (jnp.dot(widened, local_cols, preferred_element_type=jnp.float32), widened)


def route_rows(buckets, direction):
    pieces = [buckets[slot_index] for slot_index in range(len(OFFSETS))]

    def along_lat():
        for lat_step in (-1, 1):
            chosen = [
                slot_index
                for slot_index in range(len(OFFSETS))
                if OFFSETS[slot_index][0] == lat_step
            ]
            moved_stack = passed_along(
                jnp.stack([pieces[slot_index] for slot_index in chosen]),
                "lat",
                direction * lat_step,
            )
            for position, slot_index in enumerate(chosen):
                pieces[slot_index] = moved_stack[position]

    def along_lon():
        chosen = [slot_index for slot_index in range(len(OFFSETS)) if OFFSETS[slot_index][1] == 1]
        moved_stack = shifted(
            jnp.stack([pieces[slot_index] for slot_index in chosen]), "lon", direction
        )
        for position, slot_index in enumerate(chosen):
            pieces[slot_index] = moved_stack[position]

    if direction > 0:
        along_lat()
        along_lon()
    else:
        along_lon()
        along_lat()
    return jnp.stack(pieces)


def on_device(
    grid_latent,
    teacher,
    mesh_init,
    enc_weight,
    proc_weight,
    dec_weight,
    local_grid,
    local_mesh,
    local_weight,
    send_row,
    send_count,
    recv_row,
    recv_weight,
    coarse_index,
    coarse_weight,
):
    feat_width = grid_latent.shape[1]
    grid_rows = grid_latent.shape[0]
    mesh_rows = mesh_init.shape[0]
    capacity = send_row.shape[1]
    slot_ids = jnp.arange(capacity, dtype=jnp.int32)
    live_mask = (slot_ids[None, :] < send_count[:, None])[:, :, None].astype(jnp.bfloat16)

    def to_mesh(grid_values):
        local_part = jax.ops.segment_sum(
            local_weight[:, None] * grid_values[local_grid].astype(jnp.float32),
            local_mesh,
            num_segments=mesh_rows,
        )
        buckets = grid_values[send_row] * live_mask
        arrived = route_rows(buckets, 1)
        weighted = (recv_weight[:, :, None] * arrived.astype(jnp.float32)).reshape(-1, feat_width)
        remote_part = jax.ops.segment_sum(weighted, recv_row.reshape(-1), num_segments=mesh_rows)
        return local_part + remote_part

    def to_grid(mesh_values):
        local_part = jax.ops.segment_sum(
            local_weight[:, None] * mesh_values[local_mesh], local_grid, num_segments=grid_rows
        )
        messages = (recv_weight[:, :, None] * mesh_values[recv_row]).astype(jnp.bfloat16)
        arrived = route_rows(messages, -1) * live_mask
        remote_part = jax.ops.segment_sum(
            arrived.astype(jnp.float32).reshape(-1, feat_width),
            send_row.reshape(-1),
            num_segments=grid_rows,
        )
        return local_part + remote_part

    feat_index = lax.axis_index("feat")
    dec_full, proc_full, enc_full = (
        lax.all_gather(dec_weight, "feat", axis=1, tiled=True),
        lax.all_gather(proc_weight, "feat", axis=1, tiled=True),
        lax.all_gather(enc_weight, "feat", axis=1, tiled=True),
    )
    dec_rows = lax.dynamic_slice_in_dim(dec_full, feat_index * feat_width, feat_width, 0)
    proc_rows = lax.dynamic_slice_in_dim(proc_full, feat_index * feat_width, feat_width, 0)
    enc_rows = lax.dynamic_slice_in_dim(enc_full, feat_index * feat_width, feat_width, 0)
    pre_enc, grid_input = project(grid_latent, enc_weight)
    encoded = jax.nn.silu(pre_enc).astype(jnp.bfloat16)
    mesh_state = (mesh_init.astype(jnp.float32) + to_mesh(encoded)).astype(jnp.bfloat16)
    pre_proc, state_input = project(mesh_state, proc_weight)
    processed = jax.nn.silu(pre_proc).astype(jnp.bfloat16)
    coarse_all = lax.all_gather(processed[:CDEV], ("lat", "lon"), axis=0, tiled=True)
    linked = coarse_all[coarse_index].astype(jnp.float32)
    long_range = jnp.sum(coarse_weight[:, :, None] * linked, axis=1)
    updated = (mesh_state.astype(jnp.float32) + processed.astype(jnp.float32) + long_range).astype(
        jnp.bfloat16
    )
    pre_dec, updated_input = project(updated, dec_weight)
    decoded = jax.nn.silu(pre_dec)
    student = grid_latent.astype(jnp.float32) + to_grid(decoded)
    total_rows = grid_rows * lax.axis_size(("lat", "lon"))
    global_row = lax.axis_index(("lat", "lon")) * grid_rows + jnp.arange(grid_rows, dtype=jnp.int32)
    area_weight = 0.25 + jnp.sin(jnp.pi * (global_row.astype(jnp.float32) + 0.5) / total_rows)
    target = teacher.astype(jnp.float32)
    residual = student - target
    misfit, energy = lax.psum(
        (
            jnp.sum(area_weight[:, None] * residual * residual),
            jnp.sum(area_weight[:, None] * target * target),
        ),
        ("lat", "lon", "feat"),
    )
    loss_value = (misfit / energy).reshape(1)
    slope_full = 2.0 * area_weight[:, None] * residual / energy
    slope_half = slope_full.astype(jnp.bfloat16)
    back_decoded = to_mesh(slope_half)
    grad_pre_dec = (back_decoded * silu_slope(pre_dec)).astype(jnp.bfloat16)
    back_updated, grad_input = project(grad_pre_dec, dec_rows.T)
    partial_grad = jnp.dot(updated_input.T, grad_pre_dec, preferred_element_type=jnp.float32)
    grad_dec = lax.psum_scatter(partial_grad, ("lat", "lon"), scatter_dimension=0, tiled=True)
    coarse_terms = jax.ops.segment_sum(
        (coarse_weight[:, :, None] * back_updated[:, None, :]).reshape(-1, feat_width),
        coarse_index.reshape(-1),
        num_segments=coarse_all.shape[0],
    )
    coarse_share = lax.psum_scatter(coarse_terms, ("lat", "lon"), scatter_dimension=0, tiled=True)
    back_processed = back_updated + jnp.pad(
        coarse_share, ((0, mesh_rows - coarse_share.shape[0]), (0, 0))
    )
    grad_pre_proc = (back_processed * silu_slope(pre_proc)).astype(jnp.bfloat16)
    proc_back, proc_input = project(grad_pre_proc, proc_rows.T)
    back_mesh = back_updated + proc_back
    back_encoded = to_grid(back_mesh)
    grad_pre_enc = (back_encoded * silu_slope(pre_enc)).astype(jnp.bfloat16)
    enc_back, enc_input = project(grad_pre_enc, enc_rows.T)
    grad_x = (slope_full + enc_back).astype(jnp.bfloat16)
    return (loss_value, grad_x, grad_dec)


def solution(mesh):
    placed = (
        P(("groups", "lat", "lon"), "feat"),
        P(("groups", "lat", "lon"), "feat"),
        P(("groups", "lat", "lon"), "feat"),
        P(None, "feat"),
        P(None, "feat"),
        P(None, "feat"),
        P(("lat", "lon")),
        P(("lat", "lon")),
        P(("lat", "lon")),
        P(("lat", "lon"), None),
        P(("lat", "lon")),
        P(("lat", "lon"), None),
        P(("lat", "lon"), None),
        P(("lat", "lon"), None),
        P(("lat", "lon"), None),
    )
    return jax.shard_map(
        on_device,
        mesh=mesh,
        in_specs=placed,
        out_specs=(
            P("groups"),
            P(("groups", "lat", "lon"), "feat"),
            P(("groups", "lat", "lon"), "feat"),
        ),
        check_vma=False,
    )
```

profile of v0, /device:TPU:0, one launch (start us, length us, event | category | flops | bytes accessed | tf_op | source)
XLA Modules:
  0.0 457.9 jit_solution(11342208837994751582)
XLA Ops:
  8.7 0.7 fusion.45
  10.1 12.5 %all-gather.4.cloned.1.call-done = bf16[2048,512]{1,0:T(8,128)(2,1)} async-done(((bf16[2048,256]{1,0:T(8,128)(2,1)}), bf16[2048,512]{1,0:T(8,128)(2,1)}) %all-gather.4.cloned.1.call-update) | async-done | bytes 2097168 | tf_op jit(solution)/shard_map/all_gather | solution.py:29
  22.6 3.6 multiply_convert_fusion.1
  26.2 4.0 gather_fusion
  30.7 3.7 collective-permute-start.1
  34.4 1.3 collective-permute-start
  36.3 4.1 collective-permute-done.1
  40.4 4.1 collective-permute-done
  44.6 1.5 collective-permute-start.2
  46.2 19.1 %scatter_custom_fusion = f32[320,256]{1,0:T(8,128)S(1)} fusion(s32[2048]{0:T(1024)S(1)} %copy-done.14, f32[2048]{0:T(1024)S(1)} %copy-done.9, f32[]{:T(128)} %constant.24.clone.1, bf16[2048,256]{1,0:T(8,128)(2,1)S(1)} %get-tuple-element.34, s32[2048]{0:T(1024)S(1)} %fusion.43), kind=kCustom, calls=%fused_computation.34 | custom fusion | flops 1572864 | bytes 1392644 | tf_op jit(solution)/shard_map/scatter-add | solution.py:93
  65.4 10.8 %scatter_custom_fusion.1 = f32[320,256]{1,0:T(8,128)S(1)} fusion(s32[1280]{0:T(1024)S(1)} %reshape.162, bf16[1280,256]{1,0:T(8,128)(2,1)S(1)} %bitcast.30, f32[1280]{0:T(1024)S(1)} %mul.212, f32[]{:T(128)} %constant.24.clone.1), kind=kCustom, calls=%fused_computation.42 | custom fusion | flops 983040 | bytes 991236 | tf_op jit(solution)/shard_map/scatter-add | solution.py:101
  76.3 2.0 all_gather.31
  78.3 1.0 multiply_convert_fusion.6
  79.3 26.5 %all-gather = bf16[8,4,256]{2,1,0:T(4,128)(2,1)S(1)} all-gather(bf16[1,4,256]{2,1,0:T(4,128)(2,1)S(1)} %slice_bitcast_fusion), channel_id=1, replica_groups=mesh['groups'=2,'lat'=4,'lon'=2,'feat'=2] {'lat','lon'}, dimensions={0}, use_global_device_ids=true | all-gather | bytes 18432 | tf_op jit(solution)/shard_map/all_gather | solution.py:131
  105.8 2.8 gather_fusion.1
  108.9 0.9 multiply_reduce_fusion
  109.8 2.0 all_gather.33
  111.9 1.0 fusion.32
  112.9 3.1 gather_fusion.2
  116.4 11.1 %collective-permute-done.3 = bf16[3,256,256]{2,1,0:T(8,128)(2,1)S(1)} collective-permute-done((bf16[3,256,256]{2,1,0:T(8,128)(2,1)S(1)}, bf16[3,256,256]{2,1,0:T(8,128)(2,1)S(1)}, u32[]{:S(2)}, u32[]{:S(2)}) %collective-permute-start.3) | collective-permute-done | bytes 393248 | tf_op jit(solution)/shard_map/ppermute | solution.py:20
  127.6 2.2 collective-permute-start.4
  129.9 1.3 collective-permute-start.5
  131.3 21.1 %scatter_custom_fusion.2 = f32[2048,256]{1,0:T(8,128)} fusion(s32[2048]{0:T(1024)S(1)} %copy-done.15, f32[2048]{0:T(1024)S(1)} %copy-done.9, f32[]{:T(128)} %constant.24.clone.1, f32[320,256]{1,0:T(8,128)S(1)} %get-tuple-element.38, s32[2048]{0:T(1024)S(1)} %fusion.44), kind=kCustom, calls=%fused_computation.32 | custom fusion | flops 1048576 | bytes 2441220 | tf_op jit(solution)/shard_map/scatter-add | solution.py:105
  152.7 10.7 %scatter_custom_fusion.3 = f32[2048,256]{1,0:T(8,128)} fusion(s32[1280]{0:T(1024)S(1)} %reshape.178, bf16[1280,256]{1,0:T(8,128)(2,1)S(1)} %bitcast_multiply_fusion.1, f32[]{:T(128)} %constant.24.clone.1), kind=kCustom, calls=%fused_computation.46 | custom fusion | flops 655360 | bytes 2752516 | tf_op jit(solution)/shard_map/scatter-add | solution.py:110
  163.5 4.1 fusion.2
  167.6 31.5 %all-reduce.2 = (f32[]{:T(128)}, f32[]{:T(128)}) all-reduce(f32[]{:T(128)} %get-tuple-element.4, f32[]{:T(128)} %get-tuple-element.3), channel_id=1, replica_groups=mesh['groups'=2,'lat'=4,'lon'=2,'feat'=2] {'lat','lon','feat'}, use_global_device_ids=true, to_apply=%region_6.7 | all-reduce | flops 2 | bytes 16 | tf_op jit(solution)/shard_map/psum | solution.py:145
  199.1 0.9 fusion.37
  200.0 4.7 %gather_fusion.3 = bf16[1280,256]{1,0:T(8,128)(2,1)} fusion(bf16[2048,256]{1,0:T(8,128)(2,1)S(1)} %fusion.37, s32[2048]{0:T(1024)S(1)} %pad_clamp_fusion.1), kind=kCustom, calls=%fused_computation.6 | custom fusion | bytes 1315840 | tf_op jit(solution)/shard_map/gather | solution.py:98
  204.7 1.3 broadcast_multiply_fusion
  206.1 1.3 collective-permute-start.7
  207.4 1.3 collective-permute-start.6
  208.7 3.2 collective-permute-done.7
  212.6 3.5 collective-permute-done.6
  216.7 0.8 pad_maximum_fusion.3
  218.5 1.2 dynamic-slice
  220.4 3.8 all_gather.35
  224.3 4.1 all_gather.37
  228.4 19.1 %scatter_custom_fusion.4 = f32[320,256]{1,0:T(8,128)S(1)} fusion(s32[2048]{0:T(1024)S(1)} %copy-done.14, f32[2048]{0:T(1024)S(1)} %copy-done.9, f32[]{:T(128)} %constant.24.clone.1, bf16[2048,256]{1,0:T(8,128)(2,1)S(1)} %fusion.37, s32[2048]{0:T(1024)S(1)} %fusion.43), kind=kCustom, calls=%fused_computation.28 | custom fusion | flops 1572864 | bytes 1392644 | tf_op jit(solution)/shard_map/scatter-add | solution.py:93
  247.4 1.2 pad_maximum_fusion.1
  248.6 10.9 %scatter_custom_fusion.5 = f32[320,256]{1,0:T(8,128)S(1)} fusion(s32[1280]{0:T(1024)} %copy-done.16, bf16[1280,256]{1,0:T(8,128)(2,1)S(1)} %bitcast.29, f32[1280]{0:T(1024)S(1)} %mul.212, f32[]{:T(128)} %constant.24.clone.1), kind=kCustom, calls=%fused_computation.40 | custom fusion | flops 983040 | bytes 988672 | tf_op jit(solution)/shard_map/scatter-add | solution.py:101
  259.5 1.1 multiply_convert_fusion.5
  261.3 2.2 all_gather.34
  263.6 1.2 fusion.35
  264.8 1.1 mul.243
  265.9 1.5 mul.244
  267.4 7.9 %scatter_custom_fusion.6 = f32[32,256]{1,0:T(8,128)S(1)} fusion(s32[640]{0:T(1024)} %reshape.202, f32[640,256]{1,0:T(8,128)S(1)} %mul.244, f32[640]{0:T(1024)S(1)} %mul.241, f32[]{:T(128)} %constant.24.clone.1), kind=kCustom, calls=%fused_computation.62 | custom fusion | flops 327680 | bytes 691200 | tf_op jit(solution)/shard_map/scatter-add | solution.py:160
  275.3 34.9 %all-reduce.1 = f32[32,256]{1,0:T(8,128)S(1)} all-reduce(f32[32,256]{1,0:T(8,128)S(1)} %scatter_custom_fusion.6), channel_id=2, replica_groups=mesh['groups'=2,'lat'=4,'lon'=2,'feat'=2] {'lat','lon'}, use_global_device_ids=true, to_apply=%region_12.13.clone | all-reduce | flops 8192 | bytes 65536
  310.2 1.1 multiply_convert_fusion.4
  311.3 2.0 all_gather.36
  313.3 1.2 convolution_add_fusion.1
  314.6 4.1 gather_fusion.4
  318.7 1.6 multiply_convert_fusion.2
  320.4 11.1 %collective-permute-done.9 = bf16[3,256,256]{2,1,0:T(8,128)(2,1)S(1)} collective-permute-done((bf16[3,256,256]{2,1,0:T(8,128)(2,1)S(1)}, bf16[3,256,256]{2,1,0:T(8,128)(2,1)S(1)}, u32[]{:S(2)}, u32[]{:S(2)}) %collective-permute-start.9) | collective-permute-done | bytes 393248 | tf_op jit(solution)/shard_map/ppermute | solution.py:20
  331.5 0.7 pad_maximum_fusion.10
  332.2 1.3 collective-permute-start.10
  334.2 1.3 collective-permute-start.11
  335.5 21.3 %scatter_custom_fusion.7 = f32[2048,256]{1,0:T(8,128)} fusion(s32[2048]{0:T(1024)S(1)} %copy-done.15, f32[2048]{0:T(1024)S(1)} %copy-done.9, f32[]{:T(128)} %constant.24.clone.1, f32[320,256]{1,0:T(8,128)S(1)} %convolution_add_fusion.1, s32[2048]{0:T(1024)S(1)} %fusion.44), kind=kCustom, calls=%fused_computation.26 | custom fusion | flops 1048576 | bytes 2441220 | tf_op jit(solution)/shard_map/scatter-add | solution.py:105
  357.2 10.7 %scatter_custom_fusion.8 = f32[2048,256]{1,0:T(8,128)} fusion(s32[1280]{0:T(1024)} %copy-done.17, bf16[1280,256]{1,0:T(8,128)(2,1)S(1)} %bitcast_multiply_fusion, f32[]{:T(128)} %constant.24.clone.1), kind=kCustom, calls=%fused_computation.43 | custom fusion | flops 655360 | bytes 2753024 | tf_op jit(solution)/shard_map/scatter-add | solution.py:110
  367.9 4.7 %multiply_convert_fusion = bf16[2048,256]{1,0:T(8,128)(2,1)} fusion(f32[2048,256]{1,0:T(8,128)} %get-tuple-element.35, f32[2048,256]{1,0:T(8,128)} %scatter_custom_fusion.7, f32[2048,256]{1,0:T(8,128)} %scatter_custom_fusion.8), kind=kLoop, calls=%fused_computation.25 | loop fusion | flops 5242880 | bytes 7340032 | tf_op jit(solution)/shard_map/convert_element_type | solution.py:173
  372.7 1.1 fusion.63
  373.8 2.2 all_gather.39
  377.3 5.4 %all-gather.6.cloned.1.call-done = bf16[2048,512]{1,0:T(8,128)(2,1)} async-done(((bf16[2048,256]{1,0:T(8,128)(2,1)}), bf16[2048,512]{1,0:T(8,128)(2,1)}) %all-gather.6.cloned.1.call-update) | async-done | bytes 2097168 | tf_op jit(solution)/shard_map/all_gather | solution.py:29
  382.7 3.9 fusion
  386.6 63.2 %reduce-scatter.2.cloned.1.call-done = f32[64,256]{1,0:T(8,128)} async-done(((f32[512,256]{1,0:T(8,128)}), f32[64,256]{1,0:T(8,128)}) %reduce-scatter.2.cloned.1.call-update) | async-done | bytes 65552 | tf_op jit(solution)/shard_map/reduce_scatter | solution.py:159
  (116 shorter events, 8.9 us)
Async XLA Ops:
  7.2 15.4 %all-gather.4.cloned.1.call-start = ((), (), s32[]{:S(2)}) async-start(), calls=%async_computation.1 | async-start | bytes 3145728 | tf_op jit(solution)/shard_map/all_gather | solution.py:29
  7.9 374.8 %all-gather.6.cloned.1.call-start = ((), (), s32[]{:S(2)}) async-start(), calls=%async_computation.2 | async-start | bytes 3145728 | tf_op jit(solution)/shard_map/all_gather | solution.py:29
  30.3 5.5 %copy-start.13 = (s32[320,2]{0,1:T(2,128)S(1)}, s32[320,2]{0,1:T(2,128)}, u32[]{:S(2)}) copy-start(s32[320,2]{0,1:T(2,128)} %param.28) | copy-start | bytes 7684
  30.3 5.5 %copy-start.11 = (s32[5,256]{1,0:T(8,128)S(1)}, s32[5,256]{1,0:T(8,128)}, u32[]{:S(2)}) copy-start(s32[5,256]{1,0:T(8,128)} %param.26) | copy-start | bytes 15364
  30.3 5.5 %copy-start.10 = (f32[5,256]{1,0:T(8,128)S(1)}, f32[5,256]{1,0:T(8,128)}, u32[]{:S(2)}) copy-start(f32[5,256]{1,0:T(8,128)} %param.27) | copy-start | bytes 15364
  30.3 5.8 %copy-start.18 = (f32[320,2]{0,1:T(2,128)S(1)}, f32[320,2]{0,1:T(2,128)}, u32[]{:S(2)}) copy-start(f32[320,2]{0,1:T(2,128)} %param.29) | copy-start | bytes 7684
  30.6 15.6 %copy-start.15 = (s32[2048]{0:T(1024)S(1)}, s32[2048]{0:T(1024)}, u32[]{:S(2)}) copy-start(s32[2048]{0:T(1024)} %param.21) | copy-start | bytes 24580
  30.6 15.6 %copy-start.9 = (f32[2048]{0:T(1024)S(1)}, f32[2048]{0:T(1024)}, u32[]{:S(2)}) copy-start(f32[2048]{0:T(1024)} %param.23) | copy-start | bytes 24580
  30.6 15.6 %copy-start.14 = (s32[2048]{0:T(1024)S(1)}, s32[2048]{0:T(1024)}, u32[]{:S(2)}) copy-start(s32[2048]{0:T(1024)} %param.22) | copy-start | bytes 24580
  30.7 9.7 %collective-permute-start.1 = (bf16[2,256,256]{2,1,0:T(8,128)(2,1)S(1)}, bf16[2,256,256]{2,1,0:T(8,128)(2,1)S(1)}, u32[]{:S(2)}, u32[]{:S(2)}) collective-permute-start(bf16[2,256,256]{2,1,0:T(8,128)(2,1)S(1)} %pad_maximum_fusion.5), channel_id=1, source_target_pairs={{0,4},{4,8},{8,12},{1,5},{5,9},{9,13},{2,6},{6,10},{10,14},{3,7},{... | collective-permute-start | bytes 786440 | tf_op jit(solution)/shard_map/ppermute | solution.py:15
  34.4 10.1 %collective-permute-start = (bf16[2,256,256]{2,1,0:T(8,128)(2,1)S(1)}, bf16[2,256,256]{2,1,0:T(8,128)(2,1)S(1)}, u32[]{:S(2)}, u32[]{:S(2)}) collective-permute-start(bf16[2,256,256]{2,1,0:T(8,128)(2,1)S(1)} %pad_maximum_fusion.4), channel_id=1, source_target_pairs={{4,0},{8,4},{12,8},{5,1},{9,5},{13,9},{6,2},{10,6},{14,10},{7,3},{... | collective-permute-start | bytes 786440 | tf_op jit(solution)/shard_map/ppermute | solution.py:15
  35.8 29.6 %copy-start.16 = (s32[1280]{0:T(1024)}, s32[1280]{0:T(1024)S(1)}, u32[]{:S(2)}) copy-start(s32[1280]{0:T(1024)S(1)} %reshape.162) | copy-start | bytes 15364
  44.5 31.7 %copy-start.8 = (bf16[320,256]{1,0:T(8,128)(2,1)S(1)}, bf16[320,256]{1,0:T(8,128)(2,1)}, u32[]{:S(2)}) copy-start(bf16[320,256]{1,0:T(8,128)(2,1)} %param.17) | copy-start | bytes 491524
  44.6 20.7 %collective-permute-start.2 = (bf16[3,256,256]{2,1,0:T(8,128)(2,1)S(1)}, bf16[3,256,256]{2,1,0:T(8,128)(2,1)S(1)}, u32[]{:S(2)}, u32[]{:S(2)}) collective-permute-start(bf16[3,256,256]{2,1,0:T(8,128)(2,1)S(1)} %pad_maximum_fusion.2), channel_id=1, source_target_pairs={{0,2},{2,0},{1,3},{3,1},{4,6},{6,4},{5,7},{7,5},{8,10},{10,8},{9,1... | collective-permute-start | bytes 1179656 | tf_op jit(solution)/shard_map/ppermute | solution.py:20
  65.3 13.0 %copy-start.6 = (bf16[512,256]{1,0:T(8,128)(2,1)S(1)}, bf16[512,256]{1,0:T(8,128)(2,1)}, u32[]{:S(2)}) copy-start(bf16[512,256]{1,0:T(8,128)(2,1)} %param.19) | copy-start | bytes 786436
  108.6 3.3 copy-start.5
  111.9 1.0 copy-start.3
  116.0 15.2 %copy-start.12 = (s32[5,256]{1,0:T(8,128)S(1)}, s32[5,256]{1,0:T(8,128)}, u32[]{:S(2)}) copy-start(s32[5,256]{1,0:T(8,128)} %param.24) | copy-start | bytes 15364
  116.3 11.2 %collective-permute-start.3 = (bf16[3,256,256]{2,1,0:T(8,128)(2,1)S(1)}, bf16[3,256,256]{2,1,0:T(8,128)(2,1)S(1)}, u32[]{:S(2)}, u32[]{:S(2)}) collective-permute-start(bf16[3,256,256]{2,1,0:T(8,128)(2,1)S(1)} %slice.199), channel_id=1, source_target_pairs={{0,2},{2,0},{1,3},{3,1},{4,6},{6,4},{5,7},{7,5},{8,10},{10,8},{9,1... | collective-permute-start | bytes 1179656 | tf_op jit(solution)/shard_map/ppermute | solution.py:20
  127.6 24.8 %collective-permute-start.4 = (bf16[2,256,256]{2,1,0:T(8,128)(2,1)S(1)}, bf16[2,256,256]{2,1,0:T(8,128)(2,1)S(1)}, u32[]{:S(2)}, u32[]{:S(2)}) collective-permute-start(bf16[2,256,256]{2,1,0:T(8,128)(2,1)S(1)} %pad_maximum_fusion.6), channel_id=1, source_target_pairs={{0,4},{4,8},{8,12},{1,5},{5,9},{9,13},{2,6},{6,10},{10,14},{3,7},{... | collective-permute-start | bytes 786440 | tf_op jit(solution)/shard_map/ppermute | solution.py:15
  129.9 22.5 %collective-permute-start.5 = (bf16[2,256,256]{2,1,0:T(8,128)(2,1)S(1)}, bf16[2,256,256]{2,1,0:T(8,128)(2,1)S(1)}, u32[]{:S(2)}, u32[]{:S(2)}) collective-permute-start(bf16[2,256,256]{2,1,0:T(8,128)(2,1)S(1)} %pad_maximum_fusion.7), channel_id=1, source_target_pairs={{4,0},{8,4},{12,8},{5,1},{9,5},{13,9},{6,2},{10,6},{14,10},{7,3},{... | collective-permute-start | bytes 786440 | tf_op jit(solution)/shard_map/ppermute | solution.py:15
  131.2 21.5 %copy-start.17 = (s32[1280]{0:T(1024)}, s32[1280]{0:T(1024)S(1)}, u32[]{:S(2)}) copy-start(s32[1280]{0:T(1024)S(1)} %reshape.178) | copy-start | bytes 15364
  152.5 11.0 %copy-start = (bf16[2048,256]{1,0:T(8,128)(2,1)S(1)}, bf16[2048,256]{1,0:T(8,128)(2,1)}, u32[]{:S(2)}) copy-start(bf16[2048,256]{1,0:T(8,128)(2,1)} %param.15) | copy-start | bytes 3145732
  206.1 5.8 %collective-permute-start.7 = (bf16[2,256,256]{2,1,0:T(8,128)(2,1)S(1)}, bf16[2,256,256]{2,1,0:T(8,128)(2,1)S(1)}, u32[]{:S(2)}, u32[]{:S(2)}) collective-permute-start(bf16[2,256,256]{2,1,0:T(8,128)(2,1)S(1)} %pad_maximum_fusion.9), channel_id=1, source_target_pairs={{0,4},{4,8},{8,12},{1,5},{5,9},{9,13},{2,6},{6,10},{10,14},{3,7},{... | collective-permute-start | bytes 786440 | tf_op jit(solution)/shard_map/ppermute | solution.py:15
  207.4 8.6 %collective-permute-start.6 = (bf16[2,256,256]{2,1,0:T(8,128)(2,1)S(1)}, bf16[2,256,256]{2,1,0:T(8,128)(2,1)S(1)}, u32[]{:S(2)}, u32[]{:S(2)}) collective-permute-start(bf16[2,256,256]{2,1,0:T(8,128)(2,1)S(1)} %pad_maximum_fusion.8), channel_id=1, source_target_pairs={{4,0},{8,4},{12,8},{5,1},{9,5},{13,9},{6,2},{10,6},{14,10},{7,3},{... | collective-permute-start | bytes 786440 | tf_op jit(solution)/shard_map/ppermute | solution.py:15
  217.5 29.9 %collective-permute-start.8 = (bf16[3,256,256]{2,1,0:T(8,128)(2,1)}, bf16[3,256,256]{2,1,0:T(8,128)(2,1)}, u32[]{:S(2)}, u32[]{:S(2)}) collective-permute-start(bf16[3,256,256]{2,1,0:T(8,128)(2,1)} %pad_maximum_fusion.3), channel_id=1, source_target_pairs={{0,2},{2,0},{1,3},{3,1},{4,6},{6,4},{5,7},{7,5},{8,10},{10,8},{9,1... | collective-permute-start | bytes 1179656 | tf_op jit(solution)/shard_map/ppermute | solution.py:20
  260.6 0.7 copy-start.1
  320.2 11.2 %collective-permute-start.9 = (bf16[3,256,256]{2,1,0:T(8,128)(2,1)S(1)}, bf16[3,256,256]{2,1,0:T(8,128)(2,1)S(1)}, u32[]{:S(2)}, u32[]{:S(2)}) collective-permute-start(bf16[3,256,256]{2,1,0:T(8,128)(2,1)S(1)} %slice.218), channel_id=1, source_target_pairs={{0,2},{2,0},{1,3},{3,1},{4,6},{6,4},{5,7},{7,5},{8,10},{10,8},{9,1... | collective-permute-start | bytes 1179656 | tf_op jit(solution)/shard_map/ppermute | solution.py:20
  332.2 24.6 %collective-permute-start.10 = (bf16[2,256,256]{2,1,0:T(8,128)(2,1)}, bf16[2,256,256]{2,1,0:T(8,128)(2,1)S(1)}, u32[]{:S(2)}, u32[]{:S(2)}) collective-permute-start(bf16[2,256,256]{2,1,0:T(8,128)(2,1)} %pad_maximum_fusion.10), channel_id=1, source_target_pairs={{0,4},{4,8},{8,12},{1,5},{5,9},{9,13},{2,6},{6,10},{10,14},{3,7},{... | collective-permute-start | bytes 786440 | tf_op jit(solution)/shard_map/ppermute | solution.py:15
  334.2 22.6 %collective-permute-start.11 = (bf16[2,256,256]{2,1,0:T(8,128)(2,1)}, bf16[2,256,256]{2,1,0:T(8,128)(2,1)S(1)}, u32[]{:S(2)}, u32[]{:S(2)}) collective-permute-start(bf16[2,256,256]{2,1,0:T(8,128)(2,1)} %pad_maximum_fusion.11), channel_id=1, source_target_pairs={{4,0},{8,4},{12,8},{5,1},{9,5},{13,9},{6,2},{10,6},{14,10},{7,3},{... | collective-permute-start | bytes 786440 | tf_op jit(solution)/shard_map/ppermute | solution.py:15
  367.9 4.7 %copy-start.2 = (bf16[320,256]{1,0:T(8,128)(2,1)S(1)}, bf16[320,256]{1,0:T(8,128)(2,1)}, u32[]{:S(2)}) copy-start(bf16[320,256]{1,0:T(8,128)(2,1)} %copy-done.1) | copy-start | bytes 491524
  367.9 4.7 %copy-start.4 = (bf16[320,512]{1,0:T(8,128)(2,1)S(1)}, bf16[320,512]{1,0:T(8,128)(2,1)}, u32[]{:S(2)}) copy-start(bf16[320,512]{1,0:T(8,128)(2,1)} %copy-done.3) | copy-start | bytes 983044
  372.6 1.3 copy-start.7
  372.6 77.2 %reduce-scatter.2.cloned.1.call-start = ((), (), s32[]{:S(2)}) async-start(), calls=%async_computation.3 | async-start | bytes 589824 | tf_op jit(solution)/shard_map/reduce_scatter | solution.py:159
Sparse Core Ops, SparseCore 0:
  9.5 13.0 all-gather.3
  372.7 9.9 all-gather.5
  386.7 63.1 reduce-scatter.1
where the time goes:
time: 467 us; the launch traced here: 458 us
  other arithmetic  154 us (33%)
  waiting for transfers between devices  119 us (25%)
  blocking collectives  111 us (24%)
  local copies, waits for them, and re-layouts  26.8 us (6%)
  between operations  18.1 us (4%)
  starting transfers between devices  15.4 us (3%)
  matrix products  13.1 us (3%)
    reduce_scatter x1, waiting for transfers between devices, on_device(): lax.psum_scatter(partial_grad, ('lat', 'lon'), scatter_dimension=0, tiled...  63.2 us
    scatter-add x2, other arithmetic, to_grid(): jax.ops.segment_sum(local_weight[:, None] * mesh_values[local_mesh], loca...  42.4 us
    scatter-add x2, other arithmetic, to_mesh(): jax.ops.segment_sum(local_weight[:, None] * grid_values[local_grid].astyp...  38.1 us
    unnamed x1, blocking collectives  34.9 us
    psum x1, blocking collectives, on_device(): lax.psum((jnp.sum(area_weight[:, None] * residual * residual), jnp.sum(ar...  31.5 us
    all_gather x1, blocking collectives, on_device(): lax.all_gather(processed[:CDEV], ('lat', 'lon'), axis=0, tiled=True)  26.5 us
    ppermute x4, waiting for transfers between devices, shifted(): lax.ppermute(x, axis, [(i, (i + by) % length) for i in range(length)])  22.2 us
    scatter-add x2, other arithmetic, to_mesh(): jax.ops.segment_sum(weighted, recv_row.reshape(-1), num_segments=mesh_rows)  21.7 us
  transfers between devices with their start and end apart: 15, of which 9 were waited for; matrix products, arithmetic and copies ran while one was open for 20% of the time, Pallas kernels for 0%

commit v1 on v0

v1 whole, which is shorter than its diff:
```python
import functools

import jax
import jax.numpy as jnp
from jax import lax
from jax.experimental import pallas as pl
from jax.experimental.pallas import tpu as pltpu
from jax.sharding import PartitionSpec as P

CDEV = 4
PAD = 8
TILE = 256
OFFSETS = ((-1, 0), (1, 0), (-1, 1), (0, 1), (1, 1))
NB = len(OFFSETS)
MESH_ID = pl.DeviceIdType.MESH
F32 = jnp.float32
BF16 = jnp.bfloat16


def silu(v):
    return v * jax.nn.sigmoid(v)


def silu_slope(v):
    q = jax.nn.sigmoid(v)
    return q * (1.0 + v * (1.0 - q))


def nn(a, b):
    return jnp.dot(a, b, preferred_element_type=F32)


def nt(a, b):
    return lax.dot_general(a, b, (((1,), (1,)), ((), ())), preferred_element_type=F32)


def tn(a, b):
    return lax.dot_general(a, b, (((0,), (0,)), ((), ())), preferred_element_type=F32)


def iota(shape, dim):
    return lax.broadcasted_iota(jnp.int32, shape, dim)


def kernel(
    nlat, nlon, scatter_here,
    grid_ref, teach_ref, init_ref, encw_ref, procw_ref, decw_ref, area_ref,
    lg_row, lm_row, lw_row, sr_row, sr_col, rr_row, rr_col, rw_row, rw_col,
    ci_col, ci_row, cw_col, cw_row,
    loss_ref, gx_ref, gd_ref,
    xo, enco, proco, deco,
    mw, gt, am, amt, sm, smt, rm, rmt, cm, cmt,
    pre_enc, enc, slope, slope_half, gpe, gpeo, back,
    bsend, brecv,
    state, stateo, pre_proc, proc_v, upd, updo, pre_dec, gpd, gpdo, bu, bp, gpp, gppo,
    ebuf, mbuf, cbuf, tbuf, rbuf, pg, gbuf,
    psend, precv, rsend, rrecv, esend, erecv, msend, mrecv, csend, crecv, tsend, trecv, gsend, grecv,
):
    b = lax.axis_index("lat")
    o = lax.axis_index("lon")
    f = lax.axis_index("feat")
    nd = nlat * nlon * 2
    shards = nlat * nlon
    sid = b * nlon + o
    me = sid * 2 + f
    rows, width = grid_ref.shape
    mrows = init_ref.shape[0]
    cap = rr_col.shape[0] // NB
    tiles = rows // TILE
    own = pl.ds(pl.multiple_of(f * width, width), width)
    oth = pl.ds(pl.multiple_of((1 - f) * width, width), width)

    def tile(t):
        return pl.ds(pl.multiple_of(t * TILE, TILE), TILE)

    def loop(n, body, start=0):
        lax.fori_loop(start, n, lambda i, c: (body(i), c)[1], 0)

    barrier = pltpu.get_barrier_semaphore()

    def greet(r):
        d = lax.rem(me + r, nd)
        pl.semaphore_signal(
            barrier, inc=1, device_id_type=MESH_ID,
            device_id={"lat": d // (2 * nlon), "lon": lax.rem(d // 2, nlon), "feat": lax.rem(d, 2)},
        )

    loop(nd, greet, 1)
    pl.semaphore_wait(barrier, nd - 1)

    def partner(src, dst, i):
        return pltpu.make_async_remote_copy(
            src_ref=src, dst_ref=dst, send_sem=psend.at[i], recv_sem=precv.at[i],
            device_id={"feat": 1 - f}, device_id_type=MESH_ID,
        )

    def x_copy(t):
        return partner(grid_ref.at[tile(t)], xo.at[tile(t)], t)

    def g_copy(t):
        return partner(gpe.at[tile(t)], gpeo.at[tile(t)], tiles + t)

    base = 2 * tiles
    w_copies = [
        partner(decw_ref.at[oth], deco, base),
        partner(procw_ref.at[oth], proco, base + 1),
        partner(encw_ref.at[oth], enco, base + 2),
    ]
    loop(tiles, lambda t: x_copy(t).start())
    for c in w_copies:
        c.start()

    def spread(buf_from, buf_to, ss, rs, count, scatter):
        whole_group = count == nd
        mine = me if whole_group else sid

        def copy(r):
            d = lax.rem(mine + r, count)
            src = buf_from(d) if scatter else buf_from(mine)
            if whole_group:
                where = {"lat": d // (2 * nlon), "lon": lax.rem(d // 2, nlon), "feat": lax.rem(d, 2)}
            else:
                where = {"lat": d // nlon, "lon": lax.rem(d, nlon)}
            return pltpu.make_async_remote_copy(
                src_ref=src, dst_ref=buf_to.at[mine], send_sem=ss.at[d], recv_sem=rs.at[mine],
                device_id=where, device_id_type=MESH_ID,
            )

        def arrival(r):
            d = lax.rem(mine + r, count)
            return pltpu.make_async_remote_copy(
                src_ref=buf_to.at[d], dst_ref=buf_to.at[d], send_sem=ss.at[d], recv_sem=rs.at[d],
                device_id={"feat": 1 - f}, device_id_type=MESH_ID,
            )

        return (
            lambda: loop(count, lambda r: copy(r).start(), 1),
            lambda: loop(count, lambda r: arrival(r).wait_recv(), 1),
            lambda: loop(count, lambda r: copy(r).wait_send(), 1),
        )

    e_start, e_recv, e_sent = spread(lambda i: ebuf.at[i], ebuf, esend, erecv, nd, False)
    m_start, m_recv, m_sent = spread(lambda i: mbuf.at[i], mbuf, msend, mrecv, nd, False)
    c_start, c_recv, c_sent = spread(lambda i: cbuf.at[i], cbuf, csend, crecv, shards, False)
    t_start, t_recv, t_sent = spread(lambda i: tbuf.at[i], rbuf, tsend, trecv, shards, True)

    def route_copy(phase, k, direction):
        db, do = OFFSETS[k]
        return pltpu.make_async_remote_copy(
            src_ref=bsend.at[phase, k], dst_ref=brecv.at[phase, k],
            send_sem=rsend.at[phase, k], recv_sem=rrecv.at[phase, k],
            device_id={"lat": b + direction * db, "lon": lax.rem(o + direction * do + nlon, nlon)},
            device_id_type=MESH_ID,
        )

    def when_band(step, fn):
        if step == 0:
            fn()
        elif step > 0:
            pl.when(b < nlat - 1)(fn)
        else:
            pl.when(b > 0)(fn)

    def no_band(step, fn):
        if step > 0:
            pl.when(b == nlat - 1)(fn)
        elif step < 0:
            pl.when(b == 0)(fn)

    ORDER = (2, 4, 3, 0, 1)

    def route_start(phase, k, direction):
        when_band(direction * OFFSETS[k][0], lambda: route_copy(phase, k, direction).start())

    def route_recv(phase, direction):
        for k in ORDER:
            step = -direction * OFFSETS[k][0]
            when_band(step, lambda: route_copy(phase, k, direction).wait_recv())

            def clear():
                brecv[phase, k] = jnp.zeros((cap, width), BF16)

            no_band(step, clear)

    def route_sent(phase, direction):
        for k in ORDER:
            when_band(direction * OFFSETS[k][0], lambda: route_copy(phase, k, direction).wait_send())

    def energy_tile(t, acc):
        te = teach_ref[tile(t), :].astype(F32)
        return acc + jnp.sum(area_ref[tile(t), :] * te * te, axis=0, keepdims=True)

    def folded(acc):
        half = acc[:, :128]
        for i in range(1, width // 128):
            half = half + acc[:, i * 128 : (i + 1) * 128]
        return jnp.where(iota((PAD, 128), 0) == 0, half, 0.0)

    ebuf[me] = folded(lax.fori_loop(0, tiles, energy_tile, jnp.zeros((1, width), F32)))
    e_start()

    edges = lg_row.shape[1]
    MT = 64

    def build_mw(t):
        r = pl.ds(pl.multiple_of(t * MT, MT), MT)
        hit = iota((MT, edges), 0) + t * MT == lm_row[...]
        mw[r, :] = jnp.where(hit, lw_row[...], 0.0).astype(BF16)
        hit = iota((MT, NB * cap), 0) + t * MT == rr_row[...]
        rm[r, :] = jnp.where(hit, rw_row[...], 0.0).astype(BF16)

    loop(mrows // MT, build_mw)

    def build_tile(t):
        gt[...] = jnp.where(iota((TILE, edges), 0) + t * TILE == lg_row[...], 1.0, 0.0).astype(BF16)
        am[:, tile(t)] = nt(mw[...], gt[...]).astype(BF16)
        amt[tile(t), :] = nt(gt[...], mw[...]).astype(BF16)
        hit = iota((TILE, NB * cap), 0) + t * TILE == sr_row[...]
        smt[tile(t), :] = jnp.where(hit, 1.0, 0.0).astype(BF16)

    loop(tiles, build_tile)

    def build_send(k):
        r = pl.ds(pl.multiple_of(k * cap, cap), cap)
        sm[r, :] = jnp.where(iota((cap, rows), 1) == sr_col[r, :], 1.0, 0.0).astype(BF16)
        rmt[r, :] = jnp.where(iota((cap, mrows), 1) == rr_col[r, :], 1.0, 0.0).astype(BF16)

    loop(NB, build_send)
    cn = cm.shape[1]
    cmat = jnp.zeros((mrows, cn), F32)
    cmat_t = jnp.zeros((cn, mrows), F32)
    for k in range(ci_row.shape[0]):
        cmat += jnp.where(iota((mrows, cn), 1) == ci_col[:, k : k + 1], cw_col[:, k : k + 1], 0.0)
        cmat_t += jnp.where(iota((cn, mrows), 0) == ci_row[k : k + 1, :], cw_row[k : k + 1, :], 0.0)
    cm[...] = cmat.astype(BF16)
    cmt[...] = cmat_t.astype(BF16)

    def encode(t):
        x_copy(t).wait_recv()
        pre = nn(grid_ref[tile(t), :], encw_ref[own, :]) + nn(xo[tile(t), :], encw_ref[oth, :])
        pre_enc[tile(t), :] = pre
        enc[tile(t), :] = silu(pre).astype(BF16)

    loop(tiles, encode)

    def to_mesh(values, phase):
        for k in ORDER:
            bsend[phase, k] = nn(sm[k * cap : (k + 1) * cap, :], values[...]).astype(BF16)
            route_start(phase, k, 1)
        total = nn(am[...], values[...])
        bp[...] = total
        route_recv(phase, 1)
        total = bp[...]
        for k in range(NB):
            total += nn(rm[:, k * cap : (k + 1) * cap], brecv[phase, k])
        return total

    def send_messages(values, phase):
        for k in ORDER:
            r = slice(k * cap, (k + 1) * cap)
            bsend[phase, k] = (rw_col[r, :] * nn(rmt[r, :], values)).astype(BF16)
            route_start(phase, k, -1)

    def grid_sum(t, phase):
        total = None
        for k in range(NB):
            part = nn(smt[tile(t), k * cap : (k + 1) * cap], brecv[phase, k])
            total = part if total is None else total + part
        return total

    def exchanged(value, ref, other, i):
        ref[...] = value
        c = partner(ref, other, i)
        c.start()
        return c

    state_f = (init_ref[...].astype(F32) + to_mesh(enc, 0)).astype(BF16)
    c_state = exchanged(state_f, state, stateo, base + 3)
    part = nn(state[...], procw_ref[own, :])
    c_state.wait_recv()
    pre_proc[...] = part + nn(stateo[...], procw_ref[oth, :])
    proc_v[...] = silu(pre_proc[...]).astype(BF16).astype(F32)
    cbuf[sid] = proc_v[0:PAD, :]
    c_start()
    c_recv()
    linked = cbuf[...].reshape(shards * PAD, width).astype(BF16)
    updated = (state[...].astype(F32) + proc_v[...] + nn(cm[...], linked)).astype(BF16)
    c_upd = exchanged(updated, upd, updo, base + 4)
    part = nn(upd[...], decw_ref[own, :])
    c_upd.wait_recv()
    pre_dec[...] = part + nn(updo[...], decw_ref[oth, :])
    decoded = silu(pre_dec[...]).astype(BF16)
    gpp[...] = decoded
    send_messages(gpp[...], 1)

    def local_student(t):
        slope[tile(t), :] = grid_ref[tile(t), :].astype(F32) + nn(amt[tile(t), :], gpp[...])

    loop(tiles, local_student)
    e_recv()
    inv_energy = 1.0 / jnp.sum(jnp.sum(ebuf[...], axis=0), keepdims=True)
    route_recv(1, -1)

    def slope_tile(t, acc):
        student = slope[tile(t), :] + grid_sum(t, 1)
        residual = student - teach_ref[tile(t), :].astype(F32)
        weighted = area_ref[tile(t), :] * residual
        grad = 2.0 * weighted * inv_energy
        slope[tile(t), :] = grad
        slope_half[tile(t), :] = grad.astype(BF16)
        return acc + jnp.sum(weighted * residual, axis=0, keepdims=True)

    acc = lax.fori_loop(0, tiles, slope_tile, jnp.zeros((1, width), F32))
    mbuf[me] = folded(acc)

    back_decoded = to_mesh(slope_half, 2)
    c_gpd = exchanged((back_decoded * silu_slope(pre_dec[...])).astype(BF16), gpd, gpdo, base + 5)
    for c in w_copies:
        c.wait_recv()
    part = nt(gpd[...], decw_ref[own, :])
    c_gpd.wait_recv()
    bu[...] = part + nt(gpdo[...], deco[...])
    tbuf[...] = nn(cmt[...], bu[...].astype(BF16)).reshape(shards, PAD, width)
    rbuf[sid] = tbuf[sid]
    t_start()

    pg[own, :] = tn(upd[...], gpd[...])
    pg[oth, :] = tn(updo[...], gpd[...])
    t_recv()
    if scatter_here:
        share = pg.shape[0] // shards
        g_start, g_recv, g_sent = spread(
            lambda i: pg.at[pl.ds(pl.multiple_of(i * share, PAD), share)], gbuf, gsend, grecv, shards, True
        )
        gbuf[sid] = pg[pl.ds(pl.multiple_of(sid * share, PAD), share), :]

    bp[...] = bu[...]
    bp[0:PAD, :] = bu[0:PAD, :] + jnp.sum(rbuf[...], axis=0)
    c_gpp = exchanged((bp[...] * silu_slope(pre_proc[...])).astype(BF16), gpp, gppo, base + 6)
    part = bu[...] + nt(gpp[...], procw_ref[own, :])
    c_gpp.wait_recv()
    back_mesh = (part + nt(gppo[...], proco[...])).astype(BF16)
    stateo[...] = back_mesh
    send_messages(stateo[...], 3)
    if scatter_here:
        g_start()
    m_start()

    def local_back(t):
        back[tile(t), :] = nn(amt[tile(t), :], stateo[...])
        pre_enc[tile(t), :] = silu_slope(pre_enc[tile(t), :])

    loop(tiles, local_back)
    route_recv(3, -1)

    def back_tile(t):
        total = back[tile(t), :] + grid_sum(t, 3)
        gpe[tile(t), :] = (total * pre_enc[tile(t), :]).astype(BF16)
        g_copy(t).start()

    loop(tiles, back_tile)

    def grad_tile(t):
        part = slope[tile(t), :] + nt(gpe[tile(t), :], encw_ref[own, :])
        g_copy(t).wait_recv()
        gx_ref[tile(t), :] = (part + nt(gpeo[tile(t), :], enco[...])).astype(BF16)

    loop(tiles, grad_tile)
    m_recv()
    misfit = jnp.sum(jnp.sum(mbuf[...], axis=0), keepdims=True)
    loss_ref[...] = jnp.broadcast_to(misfit * inv_energy, loss_ref.shape)
    if scatter_here:
        g_recv()
        gd_ref[...] = jnp.sum(gbuf[...], axis=0)
        g_sent()
    else:
        gd_ref[...] = pg[...]

    def x_sent(t):
        x_copy(t).wait_send()
        g_copy(t).wait_send()

    loop(tiles, x_sent)
    for c in w_copies + [c_state, c_upd, c_gpd, c_gpp]:
        c.wait_send()
    route_sent(0, 1)
    route_sent(1, -1)
    route_sent(2, 1)
    route_sent(3, -1)
    for done in (e_sent, m_sent, c_sent, t_sent):
        done()


def on_device(
    nlat, nlon,
    grid_latent, teacher, mesh_init, enc_weight, proc_weight, dec_weight,
    local_grid, local_mesh, local_weight, send_row, send_count, recv_row, recv_weight,
    coarse_index, coarse_weight,
):
    rows, width = grid_latent.shape
    mrows = mesh_init.shape[0]
    full = enc_weight.shape[0]
    cap = send_row.shape[1]
    edges = local_grid.shape[0]
    shards = nlat * nlon
    nd = 2 * shards
    tiles = rows // TILE
    share = full // shards
    scatter_here = share % PAD == 0
    slots = NB * cap

    slot_ids = jnp.arange(cap, dtype=jnp.int32)
    live = slot_ids[None, :] < send_count[:, None]
    send = jnp.where(live, send_row, -1)
    coarse = (coarse_index // CDEV) * PAD + coarse_index % CDEV
    global_row = lax.axis_index(("lat", "lon")) * rows + jnp.arange(rows, dtype=jnp.int32)
    area = 0.25 + jnp.sin(jnp.pi * (global_row.astype(F32) + 0.5) / (rows * shards))

    operands = (
        grid_latent, teacher, mesh_init, enc_weight, proc_weight, dec_weight, area.reshape(rows, 1),
        local_grid.reshape(1, edges), local_mesh.reshape(1, edges), local_weight.reshape(1, edges),
        send.reshape(1, slots), send.reshape(slots, 1),
        recv_row.reshape(1, slots), recv_row.reshape(slots, 1),
        recv_weight.reshape(1, slots), recv_weight.reshape(slots, 1),
        coarse, coarse.T, coarse_weight, coarse_weight.T,
    )
    dma = pltpu.SemaphoreType.DMA
    V = pltpu.VMEM
    big = (rows, width)
    mid = (mrows, width)
    scratch = [
        V(big, BF16), V((width, width), BF16), V((width, width), BF16), V((width, width), BF16),
        V((mrows, edges), BF16), V((TILE, edges), BF16), V((mrows, rows), BF16), V((rows, mrows), BF16),
        V((slots, rows), BF16), V((rows, slots), BF16), V((mrows, slots), BF16), V((slots, mrows), BF16),
        V((mrows, PAD * shards), BF16), V((PAD * shards, mrows), BF16),
        V(big, F32), V(big, BF16), V(big, F32), V(big, BF16), V(big, BF16), V(big, BF16), V(big, F32),
        V((4, NB, cap, width), BF16), V((4, NB, cap, width), BF16),
        V(mid, BF16), V(mid, BF16), V(mid, F32), V(mid, F32), V(mid, BF16), V(mid, BF16), V(mid, F32),
        V(mid, BF16), V(mid, BF16), V(mid, F32), V(mid, F32), V(mid, BF16), V(mid, BF16),
        V((nd, PAD, 128), F32), V((nd, PAD, 128), F32), V((shards, PAD, width), F32),
        V((shards, PAD, width), F32), V((shards, PAD, width), F32),
        V((full, width), F32), V((shards, max(share, PAD), width), F32),
        dma((2 * tiles + 7,)), dma((2 * tiles + 7,)), dma((4, NB)), dma((4, NB)),
        dma((nd,)), dma((nd,)), dma((nd,)), dma((nd,)),
        dma((shards,)), dma((shards,)), dma((shards,)), dma((shards,)), dma((shards,)), dma((shards,)),
    ]
    vmem = pl.BlockSpec(memory_space=pltpu.VMEM)
    loss, grad_x, grad_dec = pl.pallas_call(
        functools.partial(kernel, nlat, nlon, scatter_here),
        out_shape=(
            jax.ShapeDtypeStruct((PAD, 128), F32),
            jax.ShapeDtypeStruct(big, BF16),
            jax.ShapeDtypeStruct((share if scatter_here else full, width), F32),
        ),
        in_specs=[vmem] * len(operands),
        out_specs=(vmem,) * 3,
        scratch_shapes=scratch,
        compiler_params=pltpu.CompilerParams(
            collective_id=0, has_side_effects=True, vmem_limit_bytes=58 * 2**20
        ),
    )(*operands)
    if not scatter_here:
        grad_dec = lax.psum_scatter(grad_dec, ("lat", "lon"), scatter_dimension=0, tiled=True)
    return (loss[0, :1], grad_x, grad_dec)


def solution(mesh):
    rows = P(("groups", "lat", "lon"), "feat")
    cols = P(None, "feat")
    flat = P(("lat", "lon"))
    table = P(("lat", "lon"), None)
    return jax.shard_map(
        functools.partial(on_device, mesh.shape["lat"], mesh.shape["lon"]),
        mesh=mesh,
        in_specs=(rows,) * 3 + (cols,) * 3 + (flat,) * 3 + (table, flat, table, table, table, table),
        out_specs=(P("groups"), rows, rows),
        check_vma=False,
    )
```

time: 467 us -> 114 us (0.24); the launches traced: 458 us -> 114 us
  other arithmetic: 154 us -> 5.04 us
  waiting for transfers between devices: 119 us -> 0 us
  blocking collectives: 111 us -> 0 us
  Pallas kernels: 0 us -> 97.2 us
  between operations: 18.1 us -> 0.73 us
  local copies, waits for them, and re-layouts: 26.8 us -> 11.1 us
  starting transfers between devices: 15.4 us -> 0 us
  matrix products: 13.1 us -> 0 us
    scatter-add x9 -> x0, other arithmetic: 132 us -> none  [the longest x2 42.4 us: to_grid(): jax.ops.segment_sum(local_weight[:, None] * mesh_values[local_mesh], loca...]
    pallas_call x0 -> x1, Pallas kernels: none -> 97.2 us  [on_device(): pl.pallas_call(functools.partial(kernel, nlat, nlon, scatter_here), out_s...]
    reduce_scatter x1 -> x0, waiting for transfers between devices: 63.2 us -> none  [on_device(): lax.psum_scatter(partial_grad, ('lat', 'lon'), scatter_dimension=0, tiled...]
    all_gather x8 -> x0, blocking collectives: 44.9 us -> none  [the longest x1 26.5 us: on_device(): lax.all_gather(processed[:CDEV], ('lat', 'lon'), axis=0, tiled=True)]
    ppermute x12 -> x0, waiting for transfers between devices: 37.1 us -> none  [the longest x4 22.2 us: shifted(): lax.ppermute(x, axis, [(i, (i + by) % length) for i in range(length)])]
    unnamed x1 -> x0, blocking collectives: 34.9 us -> none
    psum x1 -> x0, blocking collectives: 31.5 us -> none  [on_device(): lax.psum((jnp.sum(area_weight[:, None] * residual * residual), jnp.sum(ar...]
    gather x5 -> x0, local copies, waits for them, and re-layouts: 18.7 us -> none  [the longest x2 8.72 us: to_mesh(): buckets = grid_values[send_row] * live_mask]
  transfers between devices with their start and end apart: 15 -> 0, of which waited for: 9 -> 0; matrix products, arithmetic and copies ran while one was open for 20% -> 0% of each run, Pallas kernels for 0% -> 0%
where the time goes in v1:
time: 114 us
  Pallas kernels  97.2 us (85%)
  local copies, waits for them, and re-layouts  11.1 us (10%)
  other arithmetic  5.04 us (4%)
    pallas_call x1, Pallas kernels, on_device(): pl.pallas_call(functools.partial(kernel, nlat, nlon, scatter_here), out_s...  97.2 us
    unnamed x29, local copies, waits for them, and re-layouts  9.12 us
    add x1, other arithmetic, on_device(): 0.25 + jnp.sin(jnp.pi * (global_row.astype(F32) + 0.5) / (rows * shards))  4.35 us

profile of v1, /device:TPU:0, one launch (start us, length us, event | category | flops | bytes accessed | tf_op | source)
XLA Modules:
  0.0 114.1 jit_solution(2759878563961471636)
XLA Ops:
  0.6 0.0 copy-start.4
  0.6 0.0 copy-start.7
  0.7 0.7 copy-done.4
  1.3 0.6 fusion.1.ci_row
  2.0 0.0 copy-done.7
  2.0 0.0 copy-start.8
  2.0 0.0 copy-start.1
  2.0 0.0 copy-start.6
  2.0 0.7 copy-done.8
  2.7 0.0 copy-start.2
  2.7 0.0 copy-start.9
  2.7 0.0 copy-done.6
  2.7 0.6 copy-done.9
  3.3 0.1 select_bitcast_fusion
  3.4 0.0 copy-start.3
  3.4 0.0 copy-start.5
  3.4 0.8 copy.29.ci_col
  4.3 0.0 copy-done.5
  4.3 0.8 copy.30.cw_col
  5.1 0.0 copy-done.3
  5.1 1.1 copy.33
  6.2 0.0 copy-done.2
  6.2 1.1 copy.39
  7.3 0.0 copy-done.1
  7.3 1.1 copy.36
  8.4 4.3 %sine_add_fusion.area_ref = f32[2048,1]{1,0:T(8,128)} fusion(s32[]{:T(128)S(6)} %mul.16), kind=kLoop, calls=%fused_computation | loop fusion | flops 10240 | bytes 8196 | tf_op jit(solution)/shard_map/add | solution.py:417
  12.8 97.2 %shard_map.166 = (f32[8,128]{1,0:T(8,128)}, bf16[2048,256]{1,0:T(8,128)(2,1)}, f32[64,256]{1,0:T(8,128)}) custom-call(bf16[2048,256]{1,0:T(8,128)(2,1)} %grid_ref.1, bf16[2048,256]{1,0:T(8,128)(2,1)} %teach_ref.1, bf16[320,256]{1,0:T(8,128)(2,1)} %init_ref.1, bf16[512,256]{1,0:T(8,128)(2,1)} %encw_ref.1, bf16[512,256]{1,0:T(8,128)(2,1)} %procw_ref.1, ...), custom_call_target="tpu_custom_call" | custom-call | tf_op jit(solution)/shard_map/pallas_call | solution.py:448
  110.0 1.2 %slice.3 = f32[1,1]{1,0:T(1,128)} slice(f32[8,128]{1,0:T(8,128)} %get-tuple-element.6), slice={[0:1], [0:1]} | slice | bytes 8 | tf_op jit(solution)/shard_map/slice | solution.py:464
  111.1 0.0 copy-start
  111.1 2.3 %copy.42 = bf16[2048,256]{1,0:T(8,128)(2,1)} copy(bf16[2048,256]{1,0:T(8,128)(2,1)} %get-tuple-element.13) | data formatting | bytes 2097152
  113.4 0.0 copy-done
  113.4 0.6 copy.43
  (4 shorter events, 0.0 us)
Async XLA Ops:
  0.6 0.7 copy-start.4
  0.6 1.3 %copy-start.7 = (s32[5,256]{1,0:T(8,128)S(1)}, s32[5,256]{1,0:T(8,128)}, u32[]{:S(2)}) copy-start(s32[5,256]{1,0:T(8,128)} %param.26) | copy-start | bytes 15364
  2.0 0.7 copy-start.8
  2.0 5.3 %copy-start.1 = (s32[1,1,5,256]{3,1,2,0:T(1,128)}, s32[1,1,5,256]{3,1,2,0:T(1,128)S(1)}, u32[]{:S(2)}) copy-start(s32[1,1,5,256]{3,1,2,0:T(1,128)S(1)} %copy.34) | copy-start | bytes 15364
  2.0 0.7 copy-start.6
  2.7 3.6 %copy-start.2 = (f32[1,1,5,256]{3,1,2,0:T(1,128)}, f32[1,1,5,256]{3,1,2,0:T(1,128)S(1)}, u32[]{:S(2)}) copy-start(f32[1,1,5,256]{3,1,2,0:T(1,128)S(1)} %copy.37) | copy-start | bytes 15364
  2.7 0.7 copy-start.9
  3.4 1.7 %copy-start.3 = (s32[1,1,5,256]{3,1,2,0:T(1,128)}, s32[1,1,5,256]{3,1,2,0:T(1,128)S(1)}, u32[]{:S(2)}) copy-start(s32[1,1,5,256]{3,1,2,0:T(1,128)S(1)} %copy.31) | copy-start | bytes 15364
  3.4 0.8 copy-start.5
  111.1 2.3 %copy-start = (f32[64,256]{1,0:T(8,128)S(1)}, f32[64,256]{1,0:T(8,128)}, u32[]{:S(2)}) copy-start(f32[64,256]{1,0:T(8,128)} %get-tuple-element.14) | copy-start | bytes 196612

commit v2 on v1

--- a/solution.py
+++ b/solution.py
@@ -44,12 +44,11 @@
 
 def kernel(
     nlat, nlon, scatter_here,
-    grid_ref, teach_ref, init_ref, encw_ref, procw_ref, decw_ref, area_ref,
-    lg_row, lm_row, lw_row, sr_row, sr_col, rr_row, rr_col, rw_row, rw_col,
-    ci_col, ci_row, cw_col, cw_row,
+    grid_ref, teach_ref, init_ref, encw_ref, procw_ref, decw_ref,
+    lg_row, lm_row, lw_row, sr, rr, rw, ci_row, cw_row,
     loss_ref, gx_ref, gd_ref,
     xo, enco, proco, deco,
-    mw, gt, am, amt, sm, smt, rm, rmt, cm, cmt,
+    mw, gt, am, amt, sm, smt, rm, rmt, cmt, area_ref, rw_col,
     pre_enc, enc, slope, slope_half, gpe, gpeo, back,
     bsend, brecv,
     state, stateo, pre_proc, proc_v, upd, updo, pre_dec, gpd, gpdo, bu, bp, gpp, gppo,
@@ -65,13 +64,20 @@
     me = sid * 2 + f
     rows, width = grid_ref.shape
     mrows = init_ref.shape[0]
-    cap = rr_col.shape[0] // NB
+    cap = rr.shape[1]
     tiles = rows // TILE
     own = pl.ds(pl.multiple_of(f * width, width), width)
     oth = pl.ds(pl.multiple_of((1 - f) * width, width), width)
 
     def tile(t):
         return pl.ds(pl.multiple_of(t * TILE, TILE), TILE)
+
+    def column(row):
+        n = row.shape[1]
+        return jnp.sum(jnp.where(iota((n, n), 0) == iota((n, n), 1), row, 0.0), axis=1, keepdims=True)
+
+    def int_column(row):
+        return column(row.astype(F32)).astype(jnp.int32)
 
     def loop(n, body, start=0):
         lax.fori_loop(start, n, lambda i, c: (body(i), c)[1], 0)
@@ -186,7 +192,12 @@
         for k in ORDER:
             when_band(direction * OFFSETS[k][0], lambda: route_copy(phase, k, direction).wait_send())
 
+    total_rows = rows * shards
+
     def energy_tile(t, acc):
+        g = (sid * rows + t * TILE + iota((PAD, TILE), 1)).astype(F32)
+        area = 0.25 + jnp.sin(jnp.pi * (g + 0.5) / total_rows)
+        area_ref[tile(t), :] = column(area[0:1, :])
         te = teach_ref[tile(t), :].astype(F32)
         return acc + jnp.sum(area_ref[tile(t), :] * te * te, axis=0, keepdims=True)
 
@@ -202,38 +213,41 @@
     edges = lg_row.shape[1]
     MT = 64
 
+    for k in range(NB):
+        hit = iota((cap, rows), 1) == int_column(sr[k : k + 1, :])
+        sm[k * cap : (k + 1) * cap, :] = jnp.where(hit, 1.0, 0.0).astype(BF16)
+
     def build_mw(t):
         r = pl.ds(pl.multiple_of(t * MT, MT), MT)
         hit = iota((MT, edges), 0) + t * MT == lm_row[...]
         mw[r, :] = jnp.where(hit, lw_row[...], 0.0).astype(BF16)
-        hit = iota((MT, NB * cap), 0) + t * MT == rr_row[...]
-        rm[r, :] = jnp.where(hit, rw_row[...], 0.0).astype(BF16)
-
-    loop(mrows // MT, build_mw)
+        for k in range(NB):
+            hit = iota((MT, cap), 0) + t * MT == rr[k : k + 1, :]
+            rm[r, k * cap : (k + 1) * cap] = jnp.where(hit, rw[k : k + 1, :], 0.0).astype(BF16)
 
     def build_tile(t):
         gt[...] = jnp.where(iota((TILE, edges), 0) + t * TILE == lg_row[...], 1.0, 0.0).astype(BF16)
         am[:, tile(t)] = nt(mw[...], gt[...]).astype(BF16)
         amt[tile(t), :] = nt(gt[...], mw[...]).astype(BF16)
-        hit = iota((TILE, NB * cap), 0) + t * TILE == sr_row[...]
-        smt[tile(t), :] = jnp.where(hit, 1.0, 0.0).astype(BF16)
-
-    loop(tiles, build_tile)
-
-    def build_send(k):
-        r = pl.ds(pl.multiple_of(k * cap, cap), cap)
-        sm[r, :] = jnp.where(iota((cap, rows), 1) == sr_col[r, :], 1.0, 0.0).astype(BF16)
-        rmt[r, :] = jnp.where(iota((cap, mrows), 1) == rr_col[r, :], 1.0, 0.0).astype(BF16)
-
-    loop(NB, build_send)
-    cn = cm.shape[1]
-    cmat = jnp.zeros((mrows, cn), F32)
-    cmat_t = jnp.zeros((cn, mrows), F32)
-    for k in range(ci_row.shape[0]):
-        cmat += jnp.where(iota((mrows, cn), 1) == ci_col[:, k : k + 1], cw_col[:, k : k + 1], 0.0)
-        cmat_t += jnp.where(iota((cn, mrows), 0) == ci_row[k : k + 1, :], cw_row[k : k + 1, :], 0.0)
-    cm[...] = cmat.astype(BF16)
-    cmt[...] = cmat_t.astype(BF16)
+        for k in range(NB):
+            hit = iota((TILE, cap), 0) + t * TILE == sr[k : k + 1, :]
+            smt[tile(t), k * cap : (k + 1) * cap] = jnp.where(hit, 1.0, 0.0).astype(BF16)
+
+    def build_tables():
+        loop(mrows // MT, build_mw)
+        loop(tiles, build_tile)
+        for k in range(NB):
+            r = slice(k * cap, (k + 1) * cap)
+            hit = iota((cap, mrows), 1) == int_column(rr[k : k + 1, :])
+            rmt[r, :] = jnp.where(hit, 1.0, 0.0).astype(BF16)
+            rw_col[r, :] = column(rw[k : k + 1, :])
+        cn = cmt.shape[0]
+        cmat_t = jnp.zeros((cn, mrows), F32)
+        for k in range(ci_row.shape[0]):
+            j = ci_row[k : k + 1, :]
+            j = (j // CDEV) * PAD + lax.rem(j, CDEV)
+            cmat_t += jnp.where(iota((cn, mrows), 0) == j, cw_row[k : k + 1, :], 0.0)
+        cmt[...] = cmat_t.astype(BF16)
 
     def encode(t):
         x_copy(t).wait_recv()
@@ -247,6 +261,8 @@
         for k in ORDER:
             bsend[phase, k] = nn(sm[k * cap : (k + 1) * cap, :], values[...]).astype(BF16)
             route_start(phase, k, 1)
+        if phase == 0:
+            build_tables()
         total = nn(am[...], values[...])
         bp[...] = total
         route_recv(phase, 1)
@@ -284,7 +300,7 @@
     c_start()
     c_recv()
     linked = cbuf[...].reshape(shards * PAD, width).astype(BF16)
-    updated = (state[...].astype(F32) + proc_v[...] + nn(cm[...], linked)).astype(BF16)
+    updated = (state[...].astype(F32) + proc_v[...] + tn(cmt[...], linked)).astype(BF16)
     c_upd = exchanged(updated, upd, updo, base + 4)
     part = nn(upd[...], decw_ref[own, :])
     c_upd.wait_recv()
@@ -324,15 +340,16 @@
     rbuf[sid] = tbuf[sid]
     t_start()
 
-    pg[own, :] = tn(upd[...], gpd[...])
-    pg[oth, :] = tn(updo[...], gpd[...])
-    t_recv()
+    pg[own, :] = tn(upd[...], gpd[...]).astype(pg.dtype)
+    pg[oth, :] = tn(updo[...], gpd[...]).astype(pg.dtype)
     if scatter_here:
         share = pg.shape[0] // shards
         g_start, g_recv, g_sent = spread(
-            lambda i: pg.at[pl.ds(pl.multiple_of(i * share, PAD), share)], gbuf, gsend, grecv, shards, True
+            lambda i: pg.at[pl.ds(pl.multiple_of(i * share, 2 * PAD), share)], gbuf, gsend, grecv, shards, True
         )
-        gbuf[sid] = pg[pl.ds(pl.multiple_of(sid * share, PAD), share), :]
+        g_start()
+        gbuf[sid] = pg[pl.ds(pl.multiple_of(sid * share, 2 * PAD), share), :]
+    t_recv()
 
     bp[...] = bu[...]
     bp[0:PAD, :] = bu[0:PAD, :] + jnp.sum(rbuf[...], axis=0)
@@ -342,8 +359,6 @@
     back_mesh = (part + nt(gppo[...], proco[...])).astype(BF16)
     stateo[...] = back_mesh
     send_messages(stateo[...], 3)
-    if scatter_here:
-        g_start()
     m_start()
 
     def local_back(t):
@@ -368,10 +383,10 @@
     loop(tiles, grad_tile)
     m_recv()
     misfit = jnp.sum(jnp.sum(mbuf[...], axis=0), keepdims=True)
-    loss_ref[...] = jnp.broadcast_to(misfit * inv_energy, loss_ref.shape)
+    loss_ref[0] = jnp.sum(misfit * inv_energy)
     if scatter_here:
         g_recv()
-        gd_ref[...] = jnp.sum(gbuf[...], axis=0)
+        gd_ref[...] = jnp.sum(gbuf[...].astype(F32), axis=0)
         g_sent()
     else:
         gd_ref[...] = pg[...]
@@ -406,23 +421,16 @@
     nd = 2 * shards
     tiles = rows // TILE
     share = full // shards
-    scatter_here = share % PAD == 0
+    scatter_here = share % (2 * PAD) == 0
     slots = NB * cap
 
     slot_ids = jnp.arange(cap, dtype=jnp.int32)
     live = slot_ids[None, :] < send_count[:, None]
     send = jnp.where(live, send_row, -1)
-    coarse = (coarse_index // CDEV) * PAD + coarse_index % CDEV
-    global_row = lax.axis_index(("lat", "lon")) * rows + jnp.arange(rows, dtype=jnp.int32)
-    area = 0.25 + jnp.sin(jnp.pi * (global_row.astype(F32) + 0.5) / (rows * shards))
-
     operands = (
-        grid_latent, teacher, mesh_init, enc_weight, proc_weight, dec_weight, area.reshape(rows, 1),
+        grid_latent, teacher, mesh_init, enc_weight, proc_weight, dec_weight,
         local_grid.reshape(1, edges), local_mesh.reshape(1, edges), local_weight.reshape(1, edges),
-        send.reshape(1, slots), send.reshape(slots, 1),
-        recv_row.reshape(1, slots), recv_row.reshape(slots, 1),
-        recv_weight.reshape(1, slots), recv_weight.reshape(slots, 1),
-        coarse, coarse.T, coarse_weight, coarse_weight.T,
+        send, recv_row, recv_weight, coarse_index.T, coarse_weight.T,
     )
     dma = pltpu.SemaphoreType.DMA
     V = pltpu.VMEM
@@ -432,14 +440,14 @@
         V(big, BF16), V((width, width), BF16), V((width, width), BF16), V((width, width), BF16),
         V((mrows, edges), BF16), V((TILE, edges), BF16), V((mrows, rows), BF16), V((rows, mrows), BF16),
         V((slots, rows), BF16), V((rows, slots), BF16), V((mrows, slots), BF16), V((slots, mrows), BF16),
-        V((mrows, PAD * shards), BF16), V((PAD * shards, mrows), BF16),
+        V((PAD * shards, mrows), BF16), V((rows, 1), F32), V((slots, 1), F32),
         V(big, F32), V(big, BF16), V(big, F32), V(big, BF16), V(big, BF16), V(big, BF16), V(big, F32),
         V((4, NB, cap, width), BF16), V((4, NB, cap, width), BF16),
         V(mid, BF16), V(mid, BF16), V(mid, F32), V(mid, F32), V(mid, BF16), V(mid, BF16), V(mid, F32),
         V(mid, BF16), V(mid, BF16), V(mid, F32), V(mid, F32), V(mid, BF16), V(mid, BF16),
         V((nd, PAD, 128), F32), V((nd, PAD, 128), F32), V((shards, PAD, width), F32),
         V((shards, PAD, width), F32), V((shards, PAD, width), F32),
-        V((full, width), F32), V((shards, max(share, PAD), width), F32),
+        V((full, width), BF16 if scatter_here else F32), V((shards, max(share, 2 * PAD), width), BF16),
         dma((2 * tiles + 7,)), dma((2 * tiles + 7,)), dma((4, NB)), dma((4, NB)),
         dma((nd,)), dma((nd,)), dma((nd,)), dma((nd,)),
         dma((shards,)), dma((shards,)), dma((shards,)), dma((shards,)), dma((shards,)), dma((shards,)),
@@ -448,12 +456,12 @@
     loss, grad_x, grad_dec = pl.pallas_call(
         functools.partial(kernel, nlat, nlon, scatter_here),
         out_shape=(
-            jax.ShapeDtypeStruct((PAD, 128), F32),
+            jax.ShapeDtypeStruct((1,), F32),
             jax.ShapeDtypeStruct(big, BF16),
             jax.ShapeDtypeStruct((share if scatter_here else full, width), F32),
         ),
         in_specs=[vmem] * len(operands),
-        out_specs=(vmem,) * 3,
+        out_specs=(pl.BlockSpec(memory_space=pltpu.SMEM), vmem, vmem),
         scratch_shapes=scratch,
         compiler_params=pltpu.CompilerParams(
             collective_id=0, has_side_effects=True, vmem_limit_bytes=58 * 2**20
@@ -461,7 +469,7 @@
     )(*operands)
     if not scatter_here:
         grad_dec = lax.psum_scatter(grad_dec, ("lat", "lon"), scatter_dimension=0, tiled=True)
-    return (loss[0, :1], grad_x, grad_dec)
+    return (loss, grad_x, grad_dec)
 
 
 def solution(mesh):

time: 114 us -> 94.3 us (0.83)
  Pallas kernels: 97.2 us -> 86.7 us
  local copies, waits for them, and re-layouts: 11.1 us -> 3.61 us
  other arithmetic: 5.04 us -> 0.67 us
  between operations: 0.73 us -> 2.41 us
    pallas_call x1, Pallas kernels: 97.2 us -> 86.7 us  [on_device(): pl.pallas_call(functools.partial(kernel, nlat, nlon, scatter_here), out_s...]
    unnamed x29 -> x8, local copies, waits for them, and re-layouts: 9.12 us -> 3.61 us
    add x2 -> x0, other arithmetic: 4.36 us -> none  [the longest x1 4.35 us: on_device(): 0.25 + jnp.sin(jnp.pi * (global_row.astype(F32) + 0.5) / (rows * shards))]
    slice x1 -> x0, local copies, waits for them, and re-layouts: 1.19 us -> none  [on_device(): return (loss[0, :1], grad_x, grad_dec)]
where the time goes in v2:
time: 94.3 us; the launch traced here: 93.4 us
  Pallas kernels  86.7 us (92%)
  local copies, waits for them, and re-layouts  3.61 us (4%)
  between operations  2.41 us (3%)
    pallas_call x1, Pallas kernels, on_device(): pl.pallas_call(functools.partial(kernel, nlat, nlon, scatter_here), out_s...  86.7 us
    unnamed x8, local copies, waits for them, and re-layouts  3.61 us

profile of v2, /device:TPU:0, one launch (start us, length us, event | category | flops | bytes accessed | tf_op | source)
XLA Modules:
  0.0 93.4 jit_solution(7042939933786724848)
XLA Ops:
  0.6 0.0 copy-start.1
  0.6 0.0 copy-start.2
  0.6 0.7 copy-done.1
  1.3 0.0 copy-done.2
  1.3 0.7 fusion.sr
  2.0 86.7 %shard_map.166 = (f32[1]{0:T(128)}, bf16[2048,256]{1,0:T(8,128)(2,1)}, f32[64,256]{1,0:T(8,128)}) custom-call(bf16[2048,256]{1,0:T(8,128)(2,1)} %grid_ref.1, bf16[2048,256]{1,0:T(8,128)(2,1)} %teach_ref.1, bf16[320,256]{1,0:T(8,128)(2,1)} %init_ref.1, bf16[512,256]{1,0:T(8,128)(2,1)} %encw_ref.1, bf16[512,256]{1,0:T(8,128)(2,1)} %procw_ref.1, ...), custom_call_target="tpu_custom_call" | custom-call | tf_op jit(solution)/shard_map/pallas_call | solution.py:456
  89.3 0.0 copy-start
  89.3 2.3 %copy.22 = bf16[2048,256]{1,0:T(8,128)(2,1)} copy(bf16[2048,256]{1,0:T(8,128)(2,1)} %get-tuple-element.7) | data formatting | bytes 2097152
  91.6 0.0 copy-done
  91.6 0.6 copy.23
Async XLA Ops:
  0.6 0.7 copy-start.1
  0.6 0.7 copy-start.2
  89.3 2.3 %copy-start = (f32[64,256]{1,0:T(8,128)S(1)}, f32[64,256]{1,0:T(8,128)}, u32[]{:S(2)}) copy-start(f32[64,256]{1,0:T(8,128)} %get-tuple-element.8) | copy-start | bytes 196612

commit v3 on v2

--- a/solution.py
+++ b/solution.py
@@ -92,6 +92,10 @@
         )
 
     loop(nd, greet, 1)
+    for k in range(NB):
+        hit = iota((cap, rows), 1) == int_column(sr[k : k + 1, :])
+        sm[k * cap : (k + 1) * cap, :] = jnp.where(hit, 1.0, 0.0).astype(BF16)
+
     pl.semaphore_wait(barrier, nd - 1)
 
     def partner(src, dst, i):
@@ -153,7 +157,7 @@
     def route_copy(phase, k, direction):
         db, do = OFFSETS[k]
         return pltpu.make_async_remote_copy(
-            src_ref=bsend.at[phase, k], dst_ref=brecv.at[phase, k],
+            src_ref=bsend.at[phase, k], dst_ref=brecv.at[phase, pl.ds(k * cap, cap)],
             send_sem=rsend.at[phase, k], recv_sem=rrecv.at[phase, k],
             device_id={"lat": b + direction * db, "lon": lax.rem(o + direction * do + nlon, nlon)},
             device_id_type=MESH_ID,
@@ -184,7 +188,7 @@
             when_band(step, lambda: route_copy(phase, k, direction).wait_recv())
 
             def clear():
-                brecv[phase, k] = jnp.zeros((cap, width), BF16)
+                brecv[phase, k * cap : (k + 1) * cap, :] = jnp.zeros((cap, width), BF16)
 
             no_band(step, clear)
 
@@ -212,10 +216,6 @@
 
     edges = lg_row.shape[1]
     MT = 64
-
-    for k in range(NB):
-        hit = iota((cap, rows), 1) == int_column(sr[k : k + 1, :])
-        sm[k * cap : (k + 1) * cap, :] = jnp.where(hit, 1.0, 0.0).astype(BF16)
 
     def build_mw(t):
         r = pl.ds(pl.multiple_of(t * MT, MT), MT)
@@ -226,9 +226,14 @@
             rm[r, k * cap : (k + 1) * cap] = jnp.where(hit, rw[k : k + 1, :], 0.0).astype(BF16)
 
     def build_tile(t):
-        gt[...] = jnp.where(iota((TILE, edges), 0) + t * TILE == lg_row[...], 1.0, 0.0).astype(BF16)
-        am[:, tile(t)] = nt(mw[...], gt[...]).astype(BF16)
-        amt[tile(t), :] = nt(gt[...], mw[...]).astype(BF16)
+        hit = iota((TILE, edges), 0) + t * TILE == lg_row[...]
+        gt[tile(t), :] = jnp.where(hit, 1.0, 0.0).astype(BF16)
+        am[:, tile(t)] = nt(mw[...], gt[tile(t), :]).astype(BF16)
+
+    def build_back(t):
+        amt[tile(t), :] = nt(gt[tile(t), :], mw[...]).astype(BF16)
+
+    def build_arrive(t):
         for k in range(NB):
             hit = iota((TILE, cap), 0) + t * TILE == sr[k : k + 1, :]
             smt[tile(t), k * cap : (k + 1) * cap] = jnp.where(hit, 1.0, 0.0).astype(BF16)
@@ -236,11 +241,6 @@
     def build_tables():
         loop(mrows // MT, build_mw)
         loop(tiles, build_tile)
-        for k in range(NB):
-            r = slice(k * cap, (k + 1) * cap)
-            hit = iota((cap, mrows), 1) == int_column(rr[k : k + 1, :])
-            rmt[r, :] = jnp.where(hit, 1.0, 0.0).astype(BF16)
-            rw_col[r, :] = column(rw[k : k + 1, :])
         cn = cmt.shape[0]
         cmat_t = jnp.zeros((cn, mrows), F32)
         for k in range(ci_row.shape[0]):
@@ -248,6 +248,14 @@
             j = (j // CDEV) * PAD + lax.rem(j, CDEV)
             cmat_t += jnp.where(iota((cn, mrows), 0) == j, cw_row[k : k + 1, :], 0.0)
         cmt[...] = cmat_t.astype(BF16)
+
+    def build_messages():
+        for k in range(NB):
+            r = slice(k * cap, (k + 1) * cap)
+            hit = iota((cap, mrows), 1) == int_column(rr[k : k + 1, :])
+            rmt[r, :] = jnp.where(hit, 1.0, 0.0).astype(BF16)
+            rw_col[r, :] = column(rw[k : k + 1, :])
+        loop(tiles, build_arrive)
 
     def encode(t):
         x_copy(t).wait_recv()
@@ -266,10 +274,7 @@
         total = nn(am[...], values[...])
         bp[...] = total
         route_recv(phase, 1)
-        total = bp[...]
-        for k in range(NB):
-            total += nn(rm[:, k * cap : (k + 1) * cap], brecv[phase, k])
-        return total
+        return bp[...] + nn(rm[...], brecv[phase])
 
     def send_messages(values, phase):
         for k in ORDER:
@@ -278,11 +283,7 @@
             route_start(phase, k, -1)
 
     def grid_sum(t, phase):
-        total = None
-        for k in range(NB):
-            part = nn(smt[tile(t), k * cap : (k + 1) * cap], brecv[phase, k])
-            total = part if total is None else total + part
-        return total
+        return nn(smt[tile(t), :], brecv[phase])
 
     def exchanged(value, ref, other, i):
         ref[...] = value
@@ -298,6 +299,7 @@
     proc_v[...] = silu(pre_proc[...]).astype(BF16).astype(F32)
     cbuf[sid] = proc_v[0:PAD, :]
     c_start()
+    build_messages()
     c_recv()
     linked = cbuf[...].reshape(shards * PAD, width).astype(BF16)
     updated = (state[...].astype(F32) + proc_v[...] + tn(cmt[...], linked)).astype(BF16)
@@ -312,6 +314,7 @@
     def local_student(t):
         slope[tile(t), :] = grid_ref[tile(t), :].astype(F32) + nn(amt[tile(t), :], gpp[...])
 
+    loop(tiles, build_back)
     loop(tiles, local_student)
     e_recv()
     inv_energy = 1.0 / jnp.sum(jnp.sum(ebuf[...], axis=0), keepdims=True)
@@ -438,16 +441,16 @@
     mid = (mrows, width)
     scratch = [
         V(big, BF16), V((width, width), BF16), V((width, width), BF16), V((width, width), BF16),
-        V((mrows, edges), BF16), V((TILE, edges), BF16), V((mrows, rows), BF16), V((rows, mrows), BF16),
+        V((mrows, edges), BF16), V((rows, edges), BF16), V((mrows, rows), BF16), V((rows, mrows), BF16),
         V((slots, rows), BF16), V((rows, slots), BF16), V((mrows, slots), BF16), V((slots, mrows), BF16),
         V((PAD * shards, mrows), BF16), V((rows, 1), F32), V((slots, 1), F32),
         V(big, F32), V(big, BF16), V(big, F32), V(big, BF16), V(big, BF16), V(big, BF16), V(big, F32),
-        V((4, NB, cap, width), BF16), V((4, NB, cap, width), BF16),
+        V((4, NB, cap, width), BF16), V((4, slots, width), BF16),
         V(mid, BF16), V(mid, BF16), V(mid, F32), V(mid, F32), V(mid, BF16), V(mid, BF16), V(mid, F32),
         V(mid, BF16), V(mid, BF16), V(mid, F32), V(mid, F32), V(mid, BF16), V(mid, BF16),
         V((nd, PAD, 128), F32), V((nd, PAD, 128), F32), V((shards, PAD, width), F32),
         V((shards, PAD, width), F32), V((shards, PAD, width), F32),
-        V((full, width), BF16 if scatter_here else F32), V((shards, max(share, 2 * PAD), width), BF16),
+        V((full, width), BF16 if scatter_here else F32), V((shards if scatter_here else 1, max(share, 2 * PAD), width), BF16),
         dma((2 * tiles + 7,)), dma((2 * tiles + 7,)), dma((4, NB)), dma((4, NB)),
         dma((nd,)), dma((nd,)), dma((nd,)), dma((nd,)),
         dma((shards,)), dma((shards,)), dma((shards,)), dma((shards,)), dma((shards,)), dma((shards,)),
@@ -464,7 +467,7 @@
         out_specs=(pl.BlockSpec(memory_space=pltpu.SMEM), vmem, vmem),
         scratch_shapes=scratch,
         compiler_params=pltpu.CompilerParams(
-            collective_id=0, has_side_effects=True, vmem_limit_bytes=58 * 2**20
+            collective_id=0, has_side_effects=True, vmem_limit_bytes=(58 if shards <= 16 else 63) * 2**20
         ),
     )(*operands)
     if not scatter_here:

time: 94.3 us -> 90.7 us (0.962)
  Pallas kernels: 86.7 us -> 82.7 us
    pallas_call x1, Pallas kernels: 86.7 us -> 82.7 us  [on_device(): pl.pallas_call(functools.partial(kernel, nlat, nlon, scatter_here), out_s...]
where the time goes in v3:
time: 90.7 us; the launch traced here: 89.3 us
  Pallas kernels  82.7 us (91%)
  local copies, waits for them, and re-layouts  3.61 us (4%)
  between operations  2.41 us (3%)
    pallas_call x1, Pallas kernels, on_device(): pl.pallas_call(functools.partial(kernel, nlat, nlon, scatter_here), out_s...  82.7 us
    unnamed x8, local copies, waits for them, and re-layouts  3.61 us

profile of v3, /device:TPU:0, one launch (start us, length us, event | category | flops | bytes accessed | tf_op | source)
XLA Modules:
  0.0 89.3 jit_solution(12141009512260363504)
XLA Ops:
  0.6 0.0 copy-start.1
  0.6 0.0 copy-start.2
  0.6 0.7 copy-done.1
  1.3 0.0 copy-done.2
  1.3 0.7 fusion.sr
  2.0 82.7 %shard_map.166 = (f32[1]{0:T(128)}, bf16[2048,256]{1,0:T(8,128)(2,1)}, f32[64,256]{1,0:T(8,128)}) custom-call(bf16[2048,256]{1,0:T(8,128)(2,1)} %grid_ref.1, bf16[2048,256]{1,0:T(8,128)(2,1)} %teach_ref.1, bf16[320,256]{1,0:T(8,128)(2,1)} %init_ref.1, bf16[512,256]{1,0:T(8,128)(2,1)} %encw_ref.1, bf16[512,256]{1,0:T(8,128)(2,1)} %procw_ref.1, ...), custom_call_target="tpu_custom_call" | custom-call | tf_op jit(solution)/shard_map/pallas_call | solution.py:459
  85.3 0.0 copy-start
  85.3 2.3 %copy.22 = bf16[2048,256]{1,0:T(8,128)(2,1)} copy(bf16[2048,256]{1,0:T(8,128)(2,1)} %get-tuple-element.7) | data formatting | bytes 2097152
  87.6 0.0 copy-done
  87.6 0.6 copy.23
Async XLA Ops:
  0.6 0.7 copy-start.1
  0.6 0.7 copy-start.2
  85.3 2.3 %copy-start = (f32[64,256]{1,0:T(8,128)S(1)}, f32[64,256]{1,0:T(8,128)}, u32[]{:S(2)}) copy-start(f32[64,256]{1,0:T(8,128)} %get-tuple-element.8) | copy-start | bytes 196612
